TPU v7x, 32 devices: a whole 2x2x4 slice. The times are simulated.
32 devices in a mesh: energy: 16 (over z, y, x), slab: 2 (over core).
Axes of the slice: x: 2, y: 2, z: 4, core: 2. Of those that a mesh axis runs over, the one named last changes fastest.
Arguments:
- retarded: bfloat16 [16, 4, 5, 2, 384, 384], P('energy', 'slab'), may hold values from -0.09375 to 0.09375
- ballistic: float32 [16, 4, 2, 384, 384], P('energy', 'slab'), may hold values from -6 to 6
- coupling: bfloat16 [2, 384, 384], replicated, may hold values from -0.3125 to 0.3125
- occupation: float32 [2], replicated, may hold values from 0.2 to 2
- shifts: int32 [2], replicated, may hold values from 1 to 2, as said below
Outputs:
- lesser: float32 [16, 4, 2, 384, 384], P('energy', 'slab')
Inputs may be any that keep to these rules, and one draw needn't show every extreme that they name: The modes' shifts are the numbers 1 to 2 in some order.
All inputs are finite; a program needn't handle non-finite values.
Results may differ from a plain program's by a relative error of at most 0.012.
Values may be sent and summed in bfloat16 or wider, within the bound.
A program may use at most 128 MiB of HBM per device.

v0:
```python
import functools

import jax
import jax.numpy as jnp
from jax import lax
from jax.experimental import pallas as pl
from jax.experimental.pallas import tpu as pltpu
from jax.sharding import PartitionSpec as P

ITERS = 2
ROWS = 64
MESH = pl.DeviceIdType.MESH

PAIRS = ((0, 0), (1, 0), (0, 1), (1, 1), (0, 2), (0, 3), (1, 2))


def dot(a, b):
    return jnp.dot(a, b, preferred_element_type=jnp.float32)


def dot_nt(a, b):
    return lax.dot_general(a, b, (((1,), (1,)), ((), ())), preferred_element_type=jnp.float32)


def kernel(
    size, retarded, ballistic, coupling, occupation, shifts, lesser,
    base, total, own, near, far, mix_out, mix_in, mode2, band, wide, half, left, pair_c,
    base_sem, band_sem, own_send, relay_send, mix_send, wide_send,
    near_recv, far_recv, mix_recv, wide_recv, out_sem, energies,
):
    width = 2 * size
    per_block = size // ROWS
    steps = 2 * per_block
    tile = 256 if width % 256 == 0 else 128
    e = lax.axis_index("energy")
    s = lax.axis_index("slab")
    xb = e % 2
    yb = (e // 2) % 2
    d = 1 - 2 * yb
    near_dev = (e + 2 * d, s)
    relay_dev = (e + 4 * d, s)
    far_dev = (e - 4 * d, s)
    mate_dev = (e + 1 - 2 * xb, s)
    slab_dev = (e, 1 - s)
    has_relay = jnp.logical_and(e + 4 * d >= 0, e + 4 * d < energies)
    has_far = jnp.logical_and(e - 4 * d >= 0, e - 4 * d < energies)

    def block_at(slot):
        return (1 - slot) * (1 - 2 * s) + s

    def offset_at(slot, source):
        here = 2 * s + block_at(slot)
        if source % 2 == 0:
            there = 2 * s + block_at(source // 2)
        else:
            a = 1 - source // 2
            there = 2 * (1 - s) + a * (2 * s - 1) + 1 - s
        return there - here + 2

    def base_copy(slot, part):
        return pltpu.make_async_copy(
            ballistic.at[0, block_at(slot), part],
            base.at[pl.ds(slot * size, size), pl.ds(part * size, size)],
            base_sem.at[slot, part],
        )

    def band_copy(p, k):
        slot, source = PAIRS[p]
        part = (0, 1, 0)[k]
        row, col = ((0, 0), (0, 1), (1, 1))[k]
        return pltpu.make_async_copy(
            retarded.at[0, block_at(slot), offset_at(slot, source), part],
            band.at[p, pl.ds(row * size, size), pl.ds(col * size, size)],
            band_sem.at[p, k],
        )

    def rows_of(c):
        return pl.ds(pl.multiple_of(c * ROWS, ROWS), ROWS)

    def remote(src, dst, send, recv, device):
        return pltpu.make_async_remote_copy(
            src_ref=src, dst_ref=dst, send_sem=send, recv_sem=recv,
            device_id=device, device_id_type=MESH,
        )

    def own_copy(t, c):
        return remote(
            own.at[t, rows_of(c)], near.at[t, rows_of(c)],
            own_send.at[t, c], near_recv.at[t, c], near_dev,
        )

    def relay_copy(t, c):
        return remote(
            near.at[t, rows_of(c)], far.at[t, rows_of(c)],
            relay_send.at[t, c], far_recv.at[t, c], relay_dev,
        )

    def mix_copy(t, c):
        return remote(
            mix_out.at[t, rows_of(c)], mix_in.at[t, rows_of(c)],
            mix_send.at[t, c], mix_recv.at[t, c], mate_dev,
        )

    def wide_copy(t, slot):
        return remote(
            wide.at[t, 2 * slot, pl.ds(0, size)], wide.at[t, 2 * slot + 1, pl.ds(0, size)],
            wide_send.at[t, slot], wide_recv.at[t, slot], slab_dev,
        )

    for slot in range(2):
        for part in range(2):
            base_copy(slot, part).start()

    barrier = pltpu.get_barrier_semaphore()
    for device in (near_dev, mate_dev, slab_dev):
        pl.semaphore_signal(barrier, inc=1, device_id=device, device_id_type=MESH)

    @pl.when(has_relay)
    def _():
        pl.semaphore_signal(barrier, inc=1, device_id=relay_dev, device_id_type=MESH)

    @pl.when(has_far)
    def _():
        pl.semaphore_signal(barrier, inc=1, device_id=far_dev, device_id_type=MESH)

    for p in range(len(PAIRS)):
        for k in range(3):
            band_copy(p, k).start()

    first = (shifts[0] == 1)
    occ1 = jnp.where(first, occupation[0], occupation[1])
    occ2 = jnp.where(first, occupation[1], occupation[0])
    pick = jnp.where(first, 0, 1)
    pair_c[:, :size] = coupling[pick]
    pair_c[:, size:] = coupling[1 - pick]

    @pl.when(jnp.logical_not(has_far))
    def _():
        far[...] = jnp.zeros_like(far)

    own_weight = jnp.where(xb == 0, occ1, 1.0 + occ1)
    other_weight = jnp.where(xb == 0, 1.0 + occ1, occ1)
    near_weight = jnp.where(yb == 0, 1.0 + occ2, occ2)
    far_weight = jnp.where(yb == 0, occ2, 1.0 + occ2)

    for slot in range(2):
        for part in range(2):
            base_copy(slot, part).wait()
        rows = pl.ds(slot * size, size)
        own[0, rows] = base[rows].astype(jnp.bfloat16)
        if slot == 0:
            peers = 3 + has_relay.astype(jnp.int32) + has_far.astype(jnp.int32)
            pl.semaphore_wait(barrier, peers)

        @pl.loop(slot * per_block, (slot + 1) * per_block)
        def _(c):
            own_copy(0, c).start()

    for p in range(len(PAIRS)):
        for k in range(3):
            band_copy(p, k).wait()
        band[p, pl.ds(size, size), pl.ds(0, size)] = -band[p, pl.ds(0, size), pl.ds(size, size)]

    def send_mixture(t, c, other):
        rows = rows_of(c)
        mixed = own_weight * own[t, rows].astype(jnp.float32)
        mixed = mixed + other_weight * other[t, rows].astype(jnp.float32)
        mix_out[t, rows] = mixed.astype(jnp.bfloat16)
        mix_copy(t, c).start()

    def near_step(t, c):
        own_copy(t, c).wait_recv()

        @pl.when(has_relay)
        def _():
            relay_copy(t, c).start()

        @pl.when(xb == yb)
        def _():
            send_mixture(t, c, near)

    def far_step(t, c):
        @pl.when(has_far)
        def _():
            relay_copy(t, c).wait_recv()

        @pl.when(xb != yb)
        def _():
            send_mixture(t, c, far)

        rows = rows_of(c)
        mixed = near_weight * near[t, rows].astype(jnp.float32)
        mixed = mixed + far_weight * far[t, rows].astype(jnp.float32)
        mode2[rows] = mixed.astype(jnp.bfloat16)

    def step(t, c):
        near_step(t, c)
        far_step(t, c - 1)

    def widen(t, source):
        wide[t, source, size:, :size] = -wide[t, source, :size, size:]
        wide[t, source, size:, size:] = wide[t, source, :size, :size]

    def scatter(t, slot):
        @pl.loop(slot * per_block, (slot + 1) * per_block)
        def _(c):
            mix_copy(t, c).wait_recv()

        rows = pl.ds(slot * size, size)
        for part in range(2):
            cols = pl.ds(part * size, size)
            half[:size, cols] = dot_nt(mix_in[t, rows, cols], pair_c[:, :size]).astype(jnp.bfloat16)
            half[size:, cols] = dot_nt(mode2[rows, cols], pair_c[:, size:]).astype(jnp.bfloat16)

        @pl.loop(0, width // tile)
        def _(n):
            cols = pl.ds(pl.multiple_of(n * tile, tile), tile)
            wide[t, 2 * slot, :size, cols] = dot(pair_c[...], half[:, cols]).astype(jnp.bfloat16)

        wide_copy(t, slot).start()
        widen(t, 2 * slot)

    def receive(t, slot):
        wide_copy(t, slot).wait_recv()
        widen(t, 2 * slot + 1)

    def pair(t, p):
        slot, source = PAIRS[p]
        rows = pl.ds(slot * size, size)
        start = base if p < 2 else total

        @pl.loop(0, width // tile)
        def _(n):
            cols = pl.ds(pl.multiple_of(n * tile, tile), tile)
            left[:, cols] = dot(band[p, :size], wide[t, source, :, cols]).astype(jnp.bfloat16)

        @pl.loop(0, width // tile)
        def _(n):
            cols = pl.ds(pl.multiple_of(n * tile, tile), tile)
            total[rows, cols] = start[rows, cols] + dot_nt(left[...], band[p, cols])

    def out_copy(slot, part):
        return pltpu.make_async_copy(
            total.at[pl.ds(slot * size, size), pl.ds(part * size, size)],
            lesser.at[0, block_at(slot), part],
            out_sem.at[slot, part],
        )

    def finish(t, slot):
        if t == ITERS - 1:
            for part in range(2):
                out_copy(slot, part).start()
            return

        @pl.loop(slot * per_block, (slot + 1) * per_block)
        def _(c):
            own[t + 1, rows_of(c)] = total[rows_of(c)].astype(jnp.bfloat16)
            own_copy(t + 1, c).start()

    for t in range(ITERS):
        near_step(t, 0)
        lag = min(per_block + 3, steps)

        @pl.loop(1, lag)
        def _(c):
            step(t, c)

        scatter(t, 0)
        for p in range(4):
            if lag + p < steps:
                step(t, lag + p)
            if p == 2:
                receive(t, 0)
            pair(t, p)
        if lag + 4 < steps:
            @pl.loop(lag + 4, steps)
            def _(c):
                step(t, c)
        far_step(t, steps - 1)
        scatter(t, 1)
        pair(t, 4)
        receive(t, 1)
        pair(t, 5)
        finish(t, 0)
        pair(t, 6)
        finish(t, 1)

    for slot in range(2):
        for part in range(2):
            out_copy(slot, part).wait()
    for t in range(ITERS):
        for slot in range(2):
            wide_copy(t, slot).wait_send()

        @pl.loop(0, steps)
        def _(c):
            own_copy(t, c).wait_send()
            mix_copy(t, c).wait_send()

            @pl.when(has_relay)
            def _():
                relay_copy(t, c).wait_send()


def shards(energies, retarded, ballistic, coupling, occupation, shifts):
    count, blocks, _, size, _ = ballistic.shape
    assert count == 1 and blocks == 2 and energies % 4 == 0
    assert lax.axis_size("slab") == 2 and size % ROWS == 0
    width = 2 * size
    steps = 2 * size // ROWS
    blob = pltpu.VMEM((ITERS, 2 * size, width), jnp.bfloat16)
    flags = pltpu.SemaphoreType.DMA((ITERS, steps))
    pairs = len(PAIRS)
    flops = 2 * ITERS * (4 * pairs + 8) * width * width * size
    return pl.pallas_call(
        functools.partial(kernel, size, energies=energies),
        out_shape=jax.ShapeDtypeStruct(ballistic.shape, jnp.float32),
        in_specs=[
            pl.BlockSpec(memory_space=pl.ANY),
            pl.BlockSpec(memory_space=pl.ANY),
            pl.BlockSpec(memory_space=pltpu.VMEM),
            pl.BlockSpec(memory_space=pltpu.SMEM),
            pl.BlockSpec(memory_space=pltpu.SMEM),
        ],
        out_specs=pl.BlockSpec(memory_space=pl.ANY),
        scratch_shapes=[
            pltpu.VMEM((2 * size, width), jnp.float32),
            pltpu.VMEM((2 * size, width), jnp.float32),
            blob,
            blob,
            blob,
            blob,
            blob,
            pltpu.VMEM((2 * size, width), jnp.bfloat16),
            pltpu.VMEM((pairs, width, width), jnp.bfloat16),
            pltpu.VMEM((ITERS, 4, width, width), jnp.bfloat16),
            pltpu.VMEM((width, width), jnp.bfloat16),
            pltpu.VMEM((size, width), jnp.bfloat16),
            pltpu.VMEM((size, width), jnp.bfloat16),
            pltpu.SemaphoreType.DMA((2, 2)),
            pltpu.SemaphoreType.DMA((pairs, 3)),
            flags,
            flags,
            flags,
            pltpu.SemaphoreType.DMA((ITERS, 2)),
            flags,
            flags,
            flags,
            pltpu.SemaphoreType.DMA((ITERS, 2)),
            pltpu.SemaphoreType.DMA((2, 2)),
        ],
        cost_estimate=pl.CostEstimate(
            flops=flops, bytes_accessed=retarded.size * 2 + ballistic.size * 8, transcendentals=0
        ),
        compiler_params=pltpu.CompilerParams(
            collective_id=0, has_side_effects=True, vmem_limit_bytes=56 * 1024 * 1024
        ),
    )(retarded, ballistic, coupling, occupation, shifts)


def solution(mesh):
    return jax.shard_map(
        functools.partial(shards, mesh.shape["energy"]),
        mesh=mesh,
        in_specs=(
            P("energy", "slab", None, None, None, None),
            P("energy", "slab", None, None, None),
            P(),
            P(),
            P(),
        ),
        out_specs=P("energy", "slab", None, None, None),
        check_vma=False,
    )
```

profile of v0, /device:TPU:7, one launch (start us, length us, event | category | flops | bytes accessed | tf_op | source)
XLA Modules:
  0.0 104.2 jit_solution(15327321046849099286)
XLA Ops:
  0.0 101.0 %shard_map.55 = f32[1,2,2,384,384]{4,3,2,1,0:T(8,128)} custom-call(bf16[1,2,5,2,384,384]{5,4,3,2,1,0:T(8,128)(2,1)} %retarded.1, f32[1,2,2,384,384]{4,3,2,1,0:T(8,128)} %ballistic.1, bf16[2,384,384]{2,1,0:T(8,128)(2,1)} %coupling.1, f32[2]{0:T(128)} %occupation.1, s32[2]{0:T(128)} %shifts.1), custom_call_target="tpu_custom_call" | custom-call | flops 32614907904 | bytes 10616832 | tf_op jit(solution)/shard_map/pallas_call | solution.py:315
  101.0 3.2 %copy.7 = f32[1,2,2,384,384]{4,3,2,1,0:T(8,128)} copy(f32[1,2,2,384,384]{4,3,2,1,0:T(8,128)} %shard_map.55) | data formatting | bytes 4718592
where the time goes:
time: 104 us
  Pallas kernels  101 us (97%)
  local copies, waits for them, and re-layouts  3.23 us (3%)
    pallas_call x1, Pallas kernels, shards(): pl.pallas_call(functools.partial(kernel, size, energies=energies), out_sh...  101 us
    unnamed x1, local copies, waits for them, and re-layouts  3.23 us

commit v1 on v0

--- a/solution.py
+++ b/solution.py
@@ -31,7 +31,6 @@
     width = 2 * size
     per_block = size // ROWS
     steps = 2 * per_block
-    tile = 256 if width % 256 == 0 else 128
     e = lax.axis_index("energy")
     s = lax.axis_index("slab")
     xb = e % 2
@@ -211,12 +210,7 @@
             cols = pl.ds(part * size, size)
             half[:size, cols] = dot_nt(mix_in[t, rows, cols], pair_c[:, :size]).astype(jnp.bfloat16)
             half[size:, cols] = dot_nt(mode2[rows, cols], pair_c[:, size:]).astype(jnp.bfloat16)
-
-        @pl.loop(0, width // tile)
-        def _(n):
-            cols = pl.ds(pl.multiple_of(n * tile, tile), tile)
-            wide[t, 2 * slot, :size, cols] = dot(pair_c[...], half[:, cols]).astype(jnp.bfloat16)
-
+        wide[t, 2 * slot, :size] = dot(pair_c[...], half[...]).astype(jnp.bfloat16)
         wide_copy(t, slot).start()
         widen(t, 2 * slot)
 
@@ -229,15 +223,8 @@
         rows = pl.ds(slot * size, size)
         start = base if p < 2 else total
 
-        @pl.loop(0, width // tile)
-        def _(n):
-            cols = pl.ds(pl.multiple_of(n * tile, tile), tile)
-            left[:, cols] = dot(band[p, :size], wide[t, source, :, cols]).astype(jnp.bfloat16)
-
-        @pl.loop(0, width // tile)
-        def _(n):
-            cols = pl.ds(pl.multiple_of(n * tile, tile), tile)
-            total[rows, cols] = start[rows, cols] + dot_nt(left[...], band[p, cols])
+        left[...] = dot(band[p, :size], wide[t, source]).astype(jnp.bfloat16)
+        total[rows] = start[rows] + dot_nt(left[...], band[p])
 
     def out_copy(slot, part):
         return pltpu.make_async_copy(

time: 104 us -> 93.9 us (0.903)
  Pallas kernels: 101 us -> 90.2 us
    pallas_call x1, Pallas kernels: 101 us -> 90.2 us  [shards(): pl.pallas_call(functools.partial(kernel, size, energies=energies), out_sh...]
where the time goes in v1:
time: 93.9 us; the launch traced here: 93.5 us
  Pallas kernels  90.2 us (96%)
  local copies, waits for them, and re-layouts  3.23 us (3%)
    pallas_call x1, Pallas kernels, shards(): pl.pallas_call(functools.partial(kernel, size, energies=energies), out_sh...  90.2 us
    unnamed x1, local copies, waits for them, and re-layouts  3.23 us

profile of v1, /device:TPU:7, one launch (start us, length us, event | category | flops | bytes accessed | tf_op | source)
XLA Modules:
  0.0 93.5 jit_solution(16925966316464627087)
XLA Ops:
  0.0 90.2 %shard_map.55 = f32[1,2,2,384,384]{4,3,2,1,0:T(8,128)} custom-call(bf16[1,2,5,2,384,384]{5,4,3,2,1,0:T(8,128)(2,1)} %retarded.1, f32[1,2,2,384,384]{4,3,2,1,0:T(8,128)} %ballistic.1, bf16[2,384,384]{2,1,0:T(8,128)(2,1)} %coupling.1, f32[2]{0:T(128)} %occupation.1, s32[2]{0:T(128)} %shifts.1), custom_call_target="tpu_custom_call" | custom-call | flops 32614907904 | bytes 10616832 | tf_op jit(solution)/shard_map/pallas_call | solution.py:302
  90.2 3.2 %copy.7 = f32[1,2,2,384,384]{4,3,2,1,0:T(8,128)} copy(f32[1,2,2,384,384]{4,3,2,1,0:T(8,128)} %shard_map.55) | data formatting | bytes 4718592

commit v2 on v1

--- a/solution.py
+++ b/solution.py
@@ -18,13 +18,9 @@
     return jnp.dot(a, b, preferred_element_type=jnp.float32)
 
 
-def dot_nt(a, b):
-    return lax.dot_general(a, b, (((1,), (1,)), ((), ())), preferred_element_type=jnp.float32)
-
-
 def kernel(
     size, retarded, ballistic, coupling, occupation, shifts, lesser,
-    base, total, own, near, far, mix_out, mix_in, mode2, band, wide, half, left, pair_c,
+    base, total, own, near, far, mix_out, mix_in, mode2, band, turned, wide, half, left, pair_c, turned_c,
     base_sem, band_sem, own_send, relay_send, mix_send, wide_send,
     near_recv, far_recv, mix_recv, wide_recv, out_sem, energies,
 ):
@@ -63,15 +59,23 @@
             base_sem.at[slot, part],
         )
 
-    def band_copy(p, k):
+    def band_copy(p, part):
         slot, source = PAIRS[p]
-        part = (0, 1, 0)[k]
-        row, col = ((0, 0), (0, 1), (1, 1))[k]
         return pltpu.make_async_copy(
             retarded.at[0, block_at(slot), offset_at(slot, source), part],
-            band.at[p, pl.ds(row * size, size), pl.ds(col * size, size)],
-            band_sem.at[p, k],
-        )
+            band.at[p, :, pl.ds(part * size, size)],
+            band_sem.at[p, part],
+        )
+
+    def prepare(p):
+        for part in range(2):
+            band_copy(p, part).wait()
+        real = band[p, :, :size].T
+        imag = band[p, :, size:].T
+        turned[p, :size, :size] = real
+        turned[p, size:, size:] = real
+        turned[p, size:, :size] = imag
+        turned[p, :size, size:] = -imag
 
     def rows_of(c):
         return pl.ds(pl.multiple_of(c * ROWS, ROWS), ROWS)
@@ -123,8 +127,8 @@
         pl.semaphore_signal(barrier, inc=1, device_id=far_dev, device_id_type=MESH)
 
     for p in range(len(PAIRS)):
-        for k in range(3):
-            band_copy(p, k).start()
+        for part in range(2):
+            band_copy(p, part).start()
 
     first = (shifts[0] == 1)
     occ1 = jnp.where(first, occupation[0], occupation[1])
@@ -155,10 +159,8 @@
         def _(c):
             own_copy(0, c).start()
 
-    for p in range(len(PAIRS)):
-        for k in range(3):
-            band_copy(p, k).wait()
-        band[p, pl.ds(size, size), pl.ds(0, size)] = -band[p, pl.ds(0, size), pl.ds(size, size)]
+    for mode in range(2):
+        turned_c[mode] = pair_c[:, mode * size : (mode + 1) * size].T
 
     def send_mixture(t, c, other):
         rows = rows_of(c)
@@ -208,8 +210,8 @@
         rows = pl.ds(slot * size, size)
         for part in range(2):
             cols = pl.ds(part * size, size)
-            half[:size, cols] = dot_nt(mix_in[t, rows, cols], pair_c[:, :size]).astype(jnp.bfloat16)
-            half[size:, cols] = dot_nt(mode2[rows, cols], pair_c[:, size:]).astype(jnp.bfloat16)
+            half[:size, cols] = dot(mix_in[t, rows, cols], turned_c[0]).astype(jnp.bfloat16)
+            half[size:, cols] = dot(mode2[rows, cols], turned_c[1]).astype(jnp.bfloat16)
         wide[t, 2 * slot, :size] = dot(pair_c[...], half[...]).astype(jnp.bfloat16)
         wide_copy(t, slot).start()
         widen(t, 2 * slot)
@@ -223,8 +225,8 @@
         rows = pl.ds(slot * size, size)
         start = base if p < 2 else total
 
-        left[...] = dot(band[p, :size], wide[t, source]).astype(jnp.bfloat16)
-        total[rows] = start[rows] + dot_nt(left[...], band[p])
+        left[...] = dot(band[p], wide[t, source]).astype(jnp.bfloat16)
+        total[rows] = start[rows] + dot(left[...], turned[p])
 
     def out_copy(slot, part):
         return pltpu.make_async_copy(
@@ -248,7 +250,15 @@
         near_step(t, 0)
         lag = min(per_block + 3, steps)
 
-        @pl.loop(1, lag)
+        ready = 1
+        if t == 0:
+            for p in range(len(PAIRS)):
+                prepare(p)
+                if ready < lag:
+                    step(t, ready)
+                    ready += 1
+
+        @pl.loop(ready, lag)
         def _(c):
             step(t, c)
 
@@ -319,13 +329,15 @@
             blob,
             blob,
             pltpu.VMEM((2 * size, width), jnp.bfloat16),
+            pltpu.VMEM((pairs, size, width), jnp.bfloat16),
             pltpu.VMEM((pairs, width, width), jnp.bfloat16),
             pltpu.VMEM((ITERS, 4, width, width), jnp.bfloat16),
             pltpu.VMEM((width, width), jnp.bfloat16),
             pltpu.VMEM((size, width), jnp.bfloat16),
             pltpu.VMEM((size, width), jnp.bfloat16),
+            pltpu.VMEM((2, size, size), jnp.bfloat16),
             pltpu.SemaphoreType.DMA((2, 2)),
-            pltpu.SemaphoreType.DMA((pairs, 3)),
+            pltpu.SemaphoreType.DMA((pairs, 2)),
             flags,
             flags,
             flags,

time: 93.9 us -> 93.5 us (level)
  no operation moved by 1% of the time
where the time goes in v2:
time: 93.5 us; the launch traced here: 93.2 us
  Pallas kernels  90 us (96%)
  local copies, waits for them, and re-layouts  3.23 us (3%)
    pallas_call x1, Pallas kernels, shards(): pl.pallas_call(functools.partial(kernel, size, energies=energies), out_sh...  90 us
    unnamed x1, local copies, waits for them, and re-layouts  3.23 us

profile of v2, /device:TPU:7, one launch (start us, length us, event | category | flops | bytes accessed | tf_op | source)
XLA Modules:
  0.0 93.2 jit_solution(13457450539929217815)
XLA Ops:
  0.0 90.0 %shard_map.55 = f32[1,2,2,384,384]{4,3,2,1,0:T(8,128)} custom-call(bf16[1,2,5,2,384,384]{5,4,3,2,1,0:T(8,128)(2,1)} %retarded.1, f32[1,2,2,384,384]{4,3,2,1,0:T(8,128)} %ballistic.1, bf16[2,384,384]{2,1,0:T(8,128)(2,1)} %coupling.1, f32[2]{0:T(128)} %occupation.1, s32[2]{0:T(128)} %shifts.1), custom_call_target="tpu_custom_call" | custom-call | flops 32614907904 | bytes 10616832 | tf_op jit(solution)/shard_map/pallas_call | solution.py:312
  90.0 3.2 %copy.7 = f32[1,2,2,384,384]{4,3,2,1,0:T(8,128)} copy(f32[1,2,2,384,384]{4,3,2,1,0:T(8,128)} %shard_map.55) | data formatting | bytes 4718592

commit v3 on v1

--- a/solution.py
+++ b/solution.py
@@ -8,7 +8,8 @@
 from jax.sharding import PartitionSpec as P
 
 ITERS = 2
-ROWS = 64
+ROWS = 32
+AHEAD = 6
 MESH = pl.DeviceIdType.MESH
 
 PAIRS = ((0, 0), (1, 0), (0, 1), (1, 1), (0, 2), (0, 3), (1, 2))
@@ -151,9 +152,9 @@
             peers = 3 + has_relay.astype(jnp.int32) + has_far.astype(jnp.int32)
             pl.semaphore_wait(barrier, peers)
 
-        @pl.loop(slot * per_block, (slot + 1) * per_block)
-        def _(c):
-            own_copy(0, c).start()
+            @pl.loop(0, AHEAD)
+            def _(c):
+                own_copy(0, c).start()
 
     for p in range(len(PAIRS)):
         for k in range(3):
@@ -170,6 +171,10 @@
     def near_step(t, c):
         own_copy(t, c).wait_recv()
 
+        @pl.when(c + AHEAD < steps)
+        def _():
+            own_copy(t, c + AHEAD).start()
+
         @pl.when(has_relay)
         def _():
             relay_copy(t, c).start()
@@ -201,15 +206,18 @@
         wide[t, source, size:, size:] = wide[t, source, :size, :size]
 
     def scatter(t, slot):
+        rows = pl.ds(slot * size, size)
+        for part in range(2):
+            cols = pl.ds(part * size, size)
+            half[size:, cols] = dot_nt(mode2[rows, cols], pair_c[:, size:]).astype(jnp.bfloat16)
+
         @pl.loop(slot * per_block, (slot + 1) * per_block)
         def _(c):
             mix_copy(t, c).wait_recv()
 
-        rows = pl.ds(slot * size, size)
         for part in range(2):
             cols = pl.ds(part * size, size)
             half[:size, cols] = dot_nt(mix_in[t, rows, cols], pair_c[:, :size]).astype(jnp.bfloat16)
-            half[size:, cols] = dot_nt(mode2[rows, cols], pair_c[:, size:]).astype(jnp.bfloat16)
         wide[t, 2 * slot, :size] = dot(pair_c[...], half[...]).astype(jnp.bfloat16)
         wide_copy(t, slot).start()
         widen(t, 2 * slot)
@@ -239,31 +247,32 @@
                 out_copy(slot, part).start()
             return
 
-        @pl.loop(slot * per_block, (slot + 1) * per_block)
-        def _(c):
-            own[t + 1, rows_of(c)] = total[rows_of(c)].astype(jnp.bfloat16)
-            own_copy(t + 1, c).start()
+        rows = pl.ds(slot * size, size)
+        own[t + 1, rows] = total[rows].astype(jnp.bfloat16)
+        if slot == 0:
+            @pl.loop(0, AHEAD)
+            def _(c):
+                own_copy(t + 1, c).start()
 
     for t in range(ITERS):
         near_step(t, 0)
-        lag = min(per_block + 3, steps)
+        lag = (7 * steps) // 10
 
         @pl.loop(1, lag)
         def _(c):
             step(t, c)
 
         scatter(t, 0)
-        for p in range(4):
-            if lag + p < steps:
-                step(t, lag + p)
+        for p in range(3):
+            @pl.loop(lag + (steps - lag) * p // 3, lag + (steps - lag) * (p + 1) // 3)
+            def _(c):
+                step(t, c)
+
             if p == 2:
+                far_step(t, steps - 1)
                 receive(t, 0)
             pair(t, p)
-        if lag + 4 < steps:
-            @pl.loop(lag + 4, steps)
-            def _(c):
-                step(t, c)
-        far_step(t, steps - 1)
+        pair(t, 3)
         scatter(t, 1)
         pair(t, 4)
         receive(t, 1)

time: 93.9 us -> 99.2 us (1.056)
  Pallas kernels: 90.2 us -> 95.8 us
    pallas_call x1, Pallas kernels: 90.2 us -> 95.8 us  [shards(): pl.pallas_call(functools.partial(kernel, size, energies=energies), out_sh...]
where the time goes in v3:
time: 99.2 us; the launch traced here: 99.1 us
  Pallas kernels  95.8 us (97%)
  local copies, waits for them, and re-layouts  3.23 us (3%)
    pallas_call x1, Pallas kernels, shards(): pl.pallas_call(functools.partial(kernel, size, energies=energies), out_sh...  95.8 us
    unnamed x1, local copies, waits for them, and re-layouts  3.23 us

profile of v3, /device:TPU:7, one launch (start us, length us, event | category | flops | bytes accessed | tf_op | source)
XLA Modules:
  0.0 99.1 jit_solution(6162749475325263639)
XLA Ops:
  0.0 95.8 %shard_map.55 = f32[1,2,2,384,384]{4,3,2,1,0:T(8,128)} custom-call(bf16[1,2,5,2,384,384]{5,4,3,2,1,0:T(8,128)(2,1)} %retarded.1, f32[1,2,2,384,384]{4,3,2,1,0:T(8,128)} %ballistic.1, bf16[2,384,384]{2,1,0:T(8,128)(2,1)} %coupling.1, f32[2]{0:T(128)} %occupation.1, s32[2]{0:T(128)} %shifts.1), custom_call_target="tpu_custom_call" | custom-call | flops 32614907904 | bytes 10616832 | tf_op jit(solution)/shard_map/pallas_call | solution.py:311
  95.8 3.2 %copy.7 = f32[1,2,2,384,384]{4,3,2,1,0:T(8,128)} copy(f32[1,2,2,384,384]{4,3,2,1,0:T(8,128)} %shard_map.55) | data formatting | bytes 4718592

commit v4 on v1

--- a/solution.py
+++ b/solution.py
@@ -201,15 +201,18 @@
         wide[t, source, size:, size:] = wide[t, source, :size, :size]
 
     def scatter(t, slot):
+        rows = pl.ds(slot * size, size)
+        for part in range(2):
+            cols = pl.ds(part * size, size)
+            half[size:, cols] = dot_nt(mode2[rows, cols], pair_c[:, size:]).astype(jnp.bfloat16)
+
         @pl.loop(slot * per_block, (slot + 1) * per_block)
         def _(c):
             mix_copy(t, c).wait_recv()
 
-        rows = pl.ds(slot * size, size)
         for part in range(2):
             cols = pl.ds(part * size, size)
             half[:size, cols] = dot_nt(mix_in[t, rows, cols], pair_c[:, :size]).astype(jnp.bfloat16)
-            half[size:, cols] = dot_nt(mode2[rows, cols], pair_c[:, size:]).astype(jnp.bfloat16)
         wide[t, 2 * slot, :size] = dot(pair_c[...], half[...]).astype(jnp.bfloat16)
         wide_copy(t, slot).start()
         widen(t, 2 * slot)
@@ -246,31 +249,34 @@
 
     for t in range(ITERS):
         near_step(t, 0)
-        lag = min(per_block + 3, steps)
+        lag = (3 * steps) // 4
 
         @pl.loop(1, lag)
         def _(c):
             step(t, c)
 
         scatter(t, 0)
-        for p in range(4):
-            if lag + p < steps:
-                step(t, lag + p)
+        for p in range(3):
+            @pl.loop(lag + (steps - lag) * p // 3, lag + (steps - lag) * (p + 1) // 3)
+            def _(c):
+                step(t, c)
+
             if p == 2:
                 receive(t, 0)
             pair(t, p)
-        if lag + 4 < steps:
-            @pl.loop(lag + 4, steps)
-            def _(c):
-                step(t, c)
         far_step(t, steps - 1)
+        pair(t, 3)
         scatter(t, 1)
         pair(t, 4)
+        if t == ITERS - 1:
+            pair(t, 6)
+            finish(t, 1)
         receive(t, 1)
         pair(t, 5)
         finish(t, 0)
-        pair(t, 6)
-        finish(t, 1)
+        if t < ITERS - 1:
+            pair(t, 6)
+            finish(t, 1)
 
     for slot in range(2):
         for part in range(2):

time: 93.9 us -> 94.1 us (level)
  no operation moved by 1% of the time
where the time goes in v4:
time: 94.1 us; the launch traced here: 93.8 us
  Pallas kernels  90.6 us (96%)
  local copies, waits for them, and re-layouts  3.23 us (3%)
    pallas_call x1, Pallas kernels, shards(): pl.pallas_call(functools.partial(kernel, size, energies=energies), out_sh...  90.6 us
    unnamed x1, local copies, waits for them, and re-layouts  3.23 us

profile of v4, /device:TPU:7, one launch (start us, length us, event | category | flops | bytes accessed | tf_op | source)
XLA Modules:
  0.0 93.8 jit_solution(7348735449980909635)
XLA Ops:
  0.0 90.6 %shard_map.55 = f32[1,2,2,384,384]{4,3,2,1,0:T(8,128)} custom-call(bf16[1,2,5,2,384,384]{5,4,3,2,1,0:T(8,128)(2,1)} %retarded.1, f32[1,2,2,384,384]{4,3,2,1,0:T(8,128)} %ballistic.1, bf16[2,384,384]{2,1,0:T(8,128)(2,1)} %coupling.1, f32[2]{0:T(128)} %occupation.1, s32[2]{0:T(128)} %shifts.1), custom_call_target="tpu_custom_call" | custom-call | flops 32614907904 | bytes 10616832 | tf_op jit(solution)/shard_map/pallas_call | solution.py:308
  90.6 3.2 %copy.7 = f32[1,2,2,384,384]{4,3,2,1,0:T(8,128)} copy(f32[1,2,2,384,384]{4,3,2,1,0:T(8,128)} %shard_map.55) | data formatting | bytes 4718592
